TPU v7x, 512 devices: a whole 4x8x8 slice. The times are simulated.
512 devices in a mesh: rows: 32 (over x, y), tp: 16 (over z, core).
Axes of the slice: x: 4, y: 8, z: 8, core: 2. Of those that a mesh axis runs over, the one named last changes fastest.
Arguments:
- queries: bfloat16 [8192, 8192], P('rows', 'tp'), may hold values from -32 to 32
- nbr_keys: bfloat16 [32768, 8192], P(('rows', 'tp')), may hold values from -8 to 8
- nbr_values: bfloat16 [32768, 8192], P(('rows', 'tp')), may hold values from -15 to 15
- nbr_index: int32 [128, 2], P('rows'), may hold values from 0 to 7, all different within a row
- residual: bfloat16 [8192, 8192], P(('rows', 'tp')), may hold values from -2 to 2
- out_weight: bfloat16 [8192, 8192], P('tp', 'rows'), may hold values from -0.0625 to 0.0625
Outputs:
- mixed: bfloat16 [8192, 8192], P(('rows', 'tp'))
Inputs may be any that keep to these rules, and one draw needn't show every extreme that they name: `nbr_index`: the 2 entries of a span differ; they index the 8 neighbours retrieved for that span's own sequence shard.
All inputs are finite; a program needn't handle non-finite values.
Results may differ from a plain program's by a relative error of at most 0.022.
Values may be sent and summed in bfloat16 or wider, within the bound.
A program may use at most 64 MiB of HBM per device.

v0:
```python
import math
import jax
import jax.numpy as jnp
from jax import lax
from jax.sharding import PartitionSpec as P

HD = 128
CH = 64
R = 128


def shards(queries, nbr_keys, nbr_values, nbr_index, residual, out_weight):
    keys_local, values_local = (
        lax.all_to_all(nbr_keys, "tp", split_axis=1, concat_axis=0, tiled=True),
        lax.all_to_all(nbr_values, "tp", split_axis=1, concat_axis=0, tiled=True),
    )
    heads_local = queries.shape[1] // HD
    span_count = queries.shape[0] // CH
    neighbour_count = keys_local.shape[0] // R
    score_scale = 1.0 / math.sqrt(HD)
    query_blocks = queries.reshape(span_count, CH, heads_local, HD)
    key_blocks = keys_local.reshape(neighbour_count, R, heads_local, HD)[nbr_index]
    value_blocks = values_local.reshape(neighbour_count, R, heads_local, HD)[nbr_index]
    scores = (
        jnp.einsum(
            "cqhd,ckrhd->chqkr", query_blocks, key_blocks, preferred_element_type=jnp.float32
        )
        * score_scale
    )
    row_top = jnp.max(scores, axis=(3, 4), keepdims=True)
    weights = jnp.exp(scores - row_top)
    probs = (weights / jnp.sum(weights, axis=(3, 4), keepdims=True)).astype(jnp.bfloat16)
    attended = jnp.einsum(
        "chqkr,ckrhd->cqhd", probs, value_blocks, preferred_element_type=jnp.float32
    )
    attn = attended.astype(jnp.bfloat16).reshape(queries.shape[0], heads_local * HD)
    partial_value = jnp.dot(
        attn,
        lax.all_gather(out_weight, "rows", axis=1, tiled=True),
        preferred_element_type=jnp.float32,
    )
    summed = lax.psum_scatter(
        partial_value.astype(jnp.bfloat16), "tp", scatter_dimension=0, tiled=True
    ).astype(jnp.float32)
    return (residual.astype(jnp.float32) + summed).astype(jnp.bfloat16)


def solution(mesh):
    placed = (
        P("rows", "tp"),
        P(("rows", "tp"), None),
        P(("rows", "tp"), None),
        P("rows", None),
        P(("rows", "tp"), None),
        P("tp", "rows"),
    )
    return jax.shard_map(
        shards, mesh=mesh, in_specs=placed, out_specs=P(("rows", "tp"), None), check_vma=False
    )
```

profile of v0, /device:TPU:8, one launch (start us, length us, event | category | flops | bytes accessed | tf_op | source)
XLA Modules:
  0.0 204.7 jit_solution(4204165510992683133)
XLA Ops:
  6.5 0.7 all-gather.2.cloned.1.call-update
  7.3 2.3 %copy.46 = bf16[8,16,8,512]{3,2,0,1:T(8,128)(2,1)} copy(bf16[8,16,8,512]{3,2,1,0:T(8,128)(2,1)} %bitcast.35) | data formatting | bytes 2097152 | tf_op jit(solution)/shard_map/all_to_all | solution.py:14
  9.6 10.4 %all-to-all-start.1 = ((bf16[64,16,512]{2,0,1:T(8,128)(2,1)}), bf16[64,16,512]{2,0,1:T(8,128)(2,1)S(1)}, u32[]{:S(2)}, u32[]{:S(2)}) async-start(bf16[64,16,512]{2,0,1:T(8,128)(2,1)} %bitcast.29), calls=%async_computation.1 | async-start | bytes 2097152 | tf_op jit(solution)/shard_map/all_to_all | solution.py:14
  20.0 2.4 %copy.45 = bf16[8,16,8,512]{3,2,0,1:T(8,128)(2,1)} copy(bf16[8,16,8,512]{3,2,1,0:T(8,128)(2,1)} %bitcast.36) | data formatting | bytes 2097152 | tf_op jit(solution)/shard_map/all_to_all | solution.py:15
  22.4 24.3 %all-to-all-done.1 = bf16[64,16,512]{2,0,1:T(8,128)(2,1)S(1)} async-done(((bf16[64,16,512]{2,0,1:T(8,128)(2,1)}), bf16[64,16,512]{2,0,1:T(8,128)(2,1)S(1)}, u32[]{:S(2)}, u32[]{:S(2)}) %all-to-all-start.1) | async-done | bytes 1048608 | tf_op jit(solution)/shard_map/all_to_all | solution.py:14
  46.7 4.8 %all-to-all-start = ((bf16[64,16,512]{2,0,1:T(8,128)(2,1)}), bf16[64,16,512]{2,0,1:T(8,128)(2,1)S(1)}, u32[]{:S(2)}, u32[]{:S(2)}) async-start(bf16[64,16,512]{2,0,1:T(8,128)(2,1)} %bitcast.28), calls=%async_computation | async-start | bytes 2097152 | tf_op jit(solution)/shard_map/all_to_all | solution.py:15
  51.5 0.0 reduce-scatter.2.cloned.1.call-start
  51.5 0.1 copy.10
  51.6 0.1 reshape.28
  51.7 0.1 reshape.24
  51.8 0.3 reshape.23
  52.1 26.0 %all-to-all-done = bf16[64,16,512]{2,0,1:T(8,128)(2,1)S(1)} async-done(((bf16[64,16,512]{2,0,1:T(8,128)(2,1)}), bf16[64,16,512]{2,0,1:T(8,128)(2,1)S(1)}, u32[]{:S(2)}, u32[]{:S(2)}) %all-to-all-start) | async-done | bytes 1048608 | tf_op jit(solution)/shard_map/all_to_all | solution.py:15
  78.1 1.0 copy-done
  79.2 1.3 reshape.22
  80.5 1.4 gather_fusion.1
  82.0 1.4 gather_fusion
  83.4 0.6 fusion.11
  84.0 0.4 fusion.5
  84.4 0.5 fusion.2
  84.9 0.2 copy.17
  85.1 38.8 %all-gather.2.cloned.1.call-done = bf16[512,8192]{1,0:T(8,128)(2,1)} async-done(((bf16[512,256]{1,0:T(8,128)(2,1)}), bf16[512,8192]{1,0:T(8,128)(2,1)}) %all-gather.2.cloned.1.call-update) | async-done | bytes 8388624 | tf_op jit(solution)/shard_map/all_gather | solution.py:39
  123.9 7.7 %convolution_convert_fusion = bf16[256,8192]{1,0:T(8,128)(2,1)} fusion(bf16[512,8192]{1,0:T(8,128)(2,1)} %all-gather.2.cloned.1.call-done, bf16[32,8,4,128]{3,2,1,0:T(4,128)(2,1)S(1)} %bitcast.37), kind=kOutput, calls=%fused_computation.2 | convolution fusion | flops 2149580800 | bytes 12845056 | tf_op jit(solution)/shard_map/dot_general | solution.py:37
  131.7 64.5 %reduce-scatter.2.cloned.1.call-done = bf16[16,8192]{1,0:T(8,128)(2,1)} async-done(((bf16[256,8192]{1,0:T(8,128)(2,1)}), bf16[16,8192]{1,0:T(8,128)(2,1)}) %reduce-scatter.2.cloned.1.call-update) | async-done | bytes 262160 | tf_op jit(solution)/shard_map/reduce_scatter | solution.py:42
  196.2 1.7 add_convert_fusion
  (11 shorter events, 0.0 us)
Async XLA Ops:
  6.5 45.0 %copy-start.3 = (s32[4,2]{0,1:T(2,128)S(1)}, s32[4,2]{0,1:T(2,128)}, u32[]{:S(2)}) copy-start(s32[4,2]{0,1:T(2,128)} %param.9) | copy-start | bytes 100
  6.5 45.2 %copy-start.2 = (bf16[256,512]{1,0:T(8,128)(2,1)S(1)}, bf16[256,512]{1,0:T(8,128)(2,1)}, u32[]{:S(2)}) copy-start(bf16[256,512]{1,0:T(8,128)(2,1)} %param.6) | copy-start | bytes 786436
  6.5 117.4 %all-gather.2.cloned.1.call-start = ((), (), s32[]{:S(2)}) async-start(), calls=%async_computation.3 | async-start | bytes 8650752 | tf_op jit(solution)/shard_map/all_gather | solution.py:39
  9.6 37.1 %all-to-all-start.1 = ((bf16[64,16,512]{2,0,1:T(8,128)(2,1)}), bf16[64,16,512]{2,0,1:T(8,128)(2,1)S(1)}, u32[]{:S(2)}, u32[]{:S(2)}) async-start(bf16[64,16,512]{2,0,1:T(8,128)(2,1)} %bitcast.29), calls=%async_computation.1 | async-start | bytes 2097152 | tf_op jit(solution)/shard_map/all_to_all | solution.py:14
  46.7 31.5 %all-to-all-start = ((bf16[64,16,512]{2,0,1:T(8,128)(2,1)}), bf16[64,16,512]{2,0,1:T(8,128)(2,1)S(1)}, u32[]{:S(2)}, u32[]{:S(2)}) async-start(bf16[64,16,512]{2,0,1:T(8,128)(2,1)} %bitcast.28), calls=%async_computation | async-start | bytes 2097152 | tf_op jit(solution)/shard_map/all_to_all | solution.py:15
  51.5 144.7 %reduce-scatter.2.cloned.1.call-start = ((), (), s32[]{:S(2)}) async-start(), calls=%async_computation.4 | async-start | bytes 4456448 | tf_op jit(solution)/shard_map/reduce_scatter | solution.py:42
  78.1 1.1 copy-start
  123.9 72.3 %copy-start.1 = (bf16[16,8192]{1,0:T(8,128)(2,1)S(1)}, bf16[16,8192]{1,0:T(8,128)(2,1)}, u32[]{:S(2)}) copy-start(bf16[16,8192]{1,0:T(8,128)(2,1)} %param.10) | copy-start | bytes 786436
Sparse Core Ops, SparseCore 0:
  10.4 113.4 all-gather.1
  131.8 64.3 reduce-scatter.1
where the time goes:
time: 205 us
  waiting for transfers between devices  154 us (75%)
  starting transfers between devices  15.3 us (7%)
  between operations  13.5 us (7%)
  local copies, waits for them, and re-layouts  10.7 us (5%)
  matrix products  8.81 us (4%)
  other arithmetic  2.14 us (1%)
    reduce_scatter x1, waiting for transfers between devices, shards(): lax.psum_scatter(partial_value.astype(jnp.bfloat16), 'tp', scatter_dimens...  64.5 us
    all_gather x1, waiting for transfers between devices, shards(): lax.all_gather(out_weight, 'rows', axis=1, tiled=True)  38.8 us
    all_to_all x1, waiting for transfers between devices, shards(): lax.all_to_all(nbr_values, 'tp', split_axis=1, concat_axis=0, tiled=True)  26 us
    all_to_all x1, waiting for transfers between devices, shards(): lax.all_to_all(nbr_keys, 'tp', split_axis=1, concat_axis=0, tiled=True)  24.3 us
    all_to_all x1, starting transfers between devices, shards(): lax.all_to_all(nbr_keys, 'tp', split_axis=1, concat_axis=0, tiled=True)  10.4 us
    dot_general x1, matrix products, shards(): jnp.dot(attn, lax.all_gather(out_weight, 'rows', axis=1, tiled=True), pre...  7.74 us
    all_to_all x1, starting transfers between devices, shards(): lax.all_to_all(nbr_values, 'tp', split_axis=1, concat_axis=0, tiled=True)  4.79 us
  transfers between devices with their start and end apart: 4, of which 4 were waited for; matrix products, arithmetic and copies ran while one was open for 5% of the time, Pallas kernels for 0%

commit v1 on v0

--- a/solution.py
+++ b/solution.py
@@ -9,9 +9,33 @@
 R = 128
 
 
+def cut_along(x, dim, size):
+    dims = x.shape
+    tiles = x.reshape(*dims[:dim], size, dims[dim] // size, *dims[dim + 1 :])
+    return jnp.moveaxis(tiles, dim, 0)
+
+
+def laid_out(parts, dim):
+    parts = jnp.moveaxis(parts, 0, dim)
+    lengths = parts.shape
+    return parts.reshape(*lengths[:dim], lengths[dim] * lengths[dim + 1], *lengths[dim + 2 :])
+
+
+def sent_to_each(x, axis, split_dim, concat_dim):
+    size, index = (lax.axis_size(axis), lax.axis_index(axis))
+    blocks = cut_along(x, split_dim, size)
+    out = blocks
+    for hop in range(1, size):
+        target, source = ((index + hop) % size, (index - hop) % size)
+        sent = lax.dynamic_index_in_dim(blocks, target, 0)
+        partner_block = lax.ppermute(sent, axis, [(i, (i + hop) % size) for i in range(size)])
+        out = lax.dynamic_update_slice_in_dim(out, partner_block, source, axis=0)
+    return laid_out(out, concat_dim)
+
+
 def shards(queries, nbr_keys, nbr_values, nbr_index, residual, out_weight):
     keys_local, values_local = (
-        lax.all_to_all(nbr_keys, "tp", split_axis=1, concat_axis=0, tiled=True),
+        sent_to_each(nbr_keys, "tp", 1, 0),
         lax.all_to_all(nbr_values, "tp", split_axis=1, concat_axis=0, tiled=True),
     )
     heads_local = queries.shape[1] // HD

time: 205 us -> 220 us (1.073)
  the two profiles are of different devices: /device:TPU:8 before, /device:TPU:4 now
where the time goes in v1:
time: 220 us; the launch traced here: 218 us
  waiting for transfers between devices  86.9 us (40%)
  starting transfers between devices  62.3 us (28%)
  local copies, waits for them, and re-layouts  43.3 us (20%)
  between operations  14.5 us (7%)
  matrix products  8.79 us (4%)
    reduce_scatter x1, waiting for transfers between devices, shards(): lax.psum_scatter(partial_value.astype(jnp.bfloat16), 'tp', scatter_dimens...  65.9 us
    ppermute x15, starting transfers between devices, sent_to_each(): lax.ppermute(sent, axis, [(i, (i + hop) % size) for i in range(size)])  51.8 us
    dynamic_update_slice x16, local copies, waits for them, and re-layouts, sent_to_each(): out = lax.dynamic_update_slice_in_dim(out, partner_block, source, axis=0)  31.6 us
    ppermute x15, waiting for transfers between devices, sent_to_each(): lax.ppermute(sent, axis, [(i, (i + hop) % size) for i in range(size)])  20.2 us
    all_to_all x1, starting transfers between devices, shards(): lax.all_to_all(nbr_values, 'tp', split_axis=1, concat_axis=0, tiled=True)  10.4 us
    dot_general x1, matrix products, shards(): jnp.dot(attn, lax.all_gather(out_weight, 'rows', axis=1, tiled=True), pre...  7.75 us
  transfers between devices with their start and end apart: 18, of which 4 were waited for; matrix products, arithmetic and copies ran while one was open for 20% of the time, Pallas kernels for 0%

profile of v1, /device:TPU:4, one launch (start us, length us, event | category | flops | bytes accessed | tf_op | source)
XLA Modules:
  0.0 217.9 jit_solution(16254816694882183546)
XLA Ops:
  7.3 2.4 %copy.76 = bf16[8,16,8,512]{3,2,0,1:T(8,128)(2,1)} copy(bf16[8,16,8,512]{3,2,1,0:T(8,128)(2,1)} %bitcast.65) | data formatting | bytes 2097152 | tf_op jit(solution)/shard_map/all_to_all | solution.py:39
  9.7 10.4 %all-to-all-start = ((bf16[64,16,512]{2,0,1:T(8,128)(2,1)}), bf16[64,16,512]{2,0,1:T(8,128)(2,1)S(1)}, u32[]{:S(2)}, u32[]{:S(2)}) async-start(bf16[64,16,512]{2,0,1:T(8,128)(2,1)} %bitcast.58), calls=%async_computation | async-start | bytes 2097152 | tf_op jit(solution)/shard_map/all_to_all | solution.py:39
  22.0 3.1 %dynamic-slice_bitcast_fusion = (bf16[1,64,512]{2,0,1:T(2,128)(2,1)S(1)}, bf16[1,64,512]{2,0,1:T(2,128)(2,1)S(1)}, bf16[1,64,512]{2,0,1:T(2,128)(2,1)S(1)}, bf16...) fusion(bf16[64,16,512]{2,1,0:T(8,128)(2,1)S(1)} %bitcast.59, ...), kind=kLoop, calls=%fused_computation.20 | loop fusion | bytes 1966140 | tf_op jit(solution)/shard_map/jit(dynamic_index_in_dim)/dynamic_slice | solution.py:30
  25.5 3.6 %collective-permute-start.1 = (bf16[1,64,512]{2,0,1:T(2,128)(2,1)S(1)}, bf16[1,64,512]{2,0,1:T(2,128)(2,1)}, u32[]{:S(2)}, u32[]{:S(2)}) collective-permute-start(bf16[1,64,512]{2,0,1:T(2,128)(2,1)S(1)} %get-tuple-element.18), channel_id=1, source_target_pairs={{0,2},{1,3},{2,4},{3,5},{4,6},{5,7},{6,8},{7,9},{8,10},{9,11},{10,... | collective-permute-start | bytes 196616 | tf_op jit(solution)/shard_map/ppermute | solution.py:31
  29.1 4.1 %collective-permute-start.2 = (bf16[1,64,512]{2,0,1:T(2,128)(2,1)S(1)}, bf16[1,64,512]{2,0,1:T(2,128)(2,1)S(1)}, u32[]{:S(2)}, u32[]{:S(2)}) collective-permute-start(bf16[1,64,512]{2,0,1:T(2,128)(2,1)S(1)} %get-tuple-element.17), channel_id=1, source_target_pairs={{0,3},{1,4},{2,5},{3,6},{4,7},{5,8},{6,9},{7,10},{8,11},{9,12},{10... | collective-permute-start | bytes 196616 | tf_op jit(solution)/shard_map/ppermute | solution.py:31
  33.2 4.6 %collective-permute-start.3 = (bf16[1,64,512]{2,0,1:T(2,128)(2,1)S(1)}, bf16[1,64,512]{2,0,1:T(2,128)(2,1)S(1)}, u32[]{:S(2)}, u32[]{:S(2)}) collective-permute-start(bf16[1,64,512]{2,0,1:T(2,128)(2,1)S(1)} %get-tuple-element.16), channel_id=1, source_target_pairs={{0,4},{1,5},{2,6},{3,7},{4,8},{5,9},{6,10},{7,11},{8,12},{9,13},{1... | collective-permute-start | bytes 196616 | tf_op jit(solution)/shard_map/ppermute | solution.py:31
  39.9 9.4 %collective-permute-done = bf16[1,64,512]{2,0,1:T(2,128)(2,1)} collective-permute-done((bf16[1,64,512]{2,0,1:T(2,128)(2,1)S(1)}, bf16[1,64,512]{2,0,1:T(2,128)(2,1)}, u32[]{:S(2)}, u32[]{:S(2)}) %collective-permute-start) | collective-permute-done | bytes 65568 | tf_op jit(solution)/shard_map/ppermute | solution.py:31
  49.3 3.1 %collective-permute-start.5 = (bf16[1,64,512]{2,0,1:T(2,128)(2,1)}, bf16[1,64,512]{2,0,1:T(2,128)(2,1)}, u32[]{:S(2)}, u32[]{:S(2)}) collective-permute-start(bf16[1,64,512]{2,0,1:T(2,128)(2,1)} %get-tuple-element.14), channel_id=1, source_target_pairs={{0,6},{1,7},{2,8},{3,9},{4,10},{5,11},{6,12},{7,13},{8,14},{9,15},... | collective-permute-start | bytes 196616 | tf_op jit(solution)/shard_map/ppermute | solution.py:31
  52.4 2.9 %collective-permute-start.6 = (bf16[1,64,512]{2,0,1:T(2,128)(2,1)}, bf16[1,64,512]{2,0,1:T(2,128)(2,1)}, u32[]{:S(2)}, u32[]{:S(2)}) collective-permute-start(bf16[1,64,512]{2,0,1:T(2,128)(2,1)} %get-tuple-element.13), channel_id=1, source_target_pairs={{0,7},{1,8},{2,9},{3,10},{4,11},{5,12},{6,13},{7,14},{8,15},{9,0},... | collective-permute-start | bytes 196616 | tf_op jit(solution)/shard_map/ppermute | solution.py:31
  56.9 4.1 %collective-permute-start.7 = (bf16[1,64,512]{2,0,1:T(2,128)(2,1)}, bf16[1,64,512]{2,0,1:T(2,128)(2,1)}, u32[]{:S(2)}, u32[]{:S(2)}) collective-permute-start(bf16[1,64,512]{2,0,1:T(2,128)(2,1)} %get-tuple-element.12), channel_id=1, source_target_pairs={{0,8},{1,9},{2,10},{3,11},{4,12},{5,13},{6,14},{7,15},{8,0},{9,1},... | collective-permute-start | bytes 196616 | tf_op jit(solution)/shard_map/ppermute | solution.py:31
  61.0 6.2 %collective-permute-start.8 = (bf16[1,64,512]{2,0,1:T(2,128)(2,1)S(1)}, bf16[1,64,512]{2,0,1:T(2,128)(2,1)}, u32[]{:S(2)}, u32[]{:S(2)}) collective-permute-start(bf16[1,64,512]{2,0,1:T(2,128)(2,1)S(1)} %get-tuple-element.11), channel_id=1, source_target_pairs={{0,9},{1,10},{2,11},{3,12},{4,13},{5,14},{6,15},{7,0},{8,1},{9,2},... | collective-permute-start | bytes 196616 | tf_op jit(solution)/shard_map/ppermute | solution.py:31
  67.1 9.2 %collective-permute-done.4 = bf16[1,64,512]{2,0,1:T(2,128)(2,1)S(1)} collective-permute-done((bf16[1,64,512]{2,0,1:T(2,128)(2,1)S(1)}, bf16[1,64,512]{2,0,1:T(2,128)(2,1)S(1)}, u32[]{:S(2)}, u32[]{:S(2)}) %collective-permute-start.4) | collective-permute-done | bytes 65568 | tf_op jit(solution)/shard_map/ppermute | solution.py:31
  77.0 3.4 %collective-permute-start.9 = (bf16[1,64,512]{2,0,1:T(2,128)(2,1)S(1)}, bf16[1,64,512]{2,0,1:T(2,128)(2,1)}, u32[]{:S(2)}, u32[]{:S(2)}) collective-permute-start(bf16[1,64,512]{2,0,1:T(2,128)(2,1)S(1)} %get-tuple-element.10), channel_id=1, source_target_pairs={{0,10},{1,11},{2,12},{3,13},{4,14},{5,15},{6,0},{7,1},{8,2},{9,3},... | collective-permute-start | bytes 196616 | tf_op jit(solution)/shard_map/ppermute | solution.py:31
  81.0 5.1 %collective-permute-start.10 = (bf16[1,64,512]{2,0,1:T(2,128)(2,1)S(1)}, bf16[1,64,512]{2,0,1:T(2,128)(2,1)S(1)}, u32[]{:S(2)}, u32[]{:S(2)}) collective-permute-start(bf16[1,64,512]{2,0,1:T(2,128)(2,1)S(1)} %get-tuple-element.9), channel_id=1, source_target_pairs={{0,11},{1,12},{2,13},{3,14},{4,15},{5,0},{6,1},{7,2},{8,3},{9,4},{... | collective-permute-start | bytes 196616 | tf_op jit(solution)/shard_map/ppermute | solution.py:31
  86.2 7.8 %collective-permute-start.11 = (bf16[1,64,512]{2,0,1:T(2,128)(2,1)S(1)}, bf16[1,64,512]{2,0,1:T(2,128)(2,1)S(1)}, u32[]{:S(2)}, u32[]{:S(2)}) collective-permute-start(bf16[1,64,512]{2,0,1:T(2,128)(2,1)S(1)} %get-tuple-element.8), channel_id=1, source_target_pairs={{0,12},{1,13},{2,14},{3,15},{4,0},{5,1},{6,2},{7,3},{8,4},{9,5},{1... | collective-permute-start | bytes 196616 | tf_op jit(solution)/shard_map/ppermute | solution.py:31
  101.0 2.4 %dynamic_update_slice.46 = bf16[16,64,512]{2,0,1:T(8,128)(2,1)S(1)} dynamic-update-slice(bf16[16,64,512]{2,0,1:T(8,128)(2,1)S(1)} %dynamic_update_slice.45, bf16[1,64,512]{2,0,1:T(2,128)(2,1)} %collective-permute-done.1, s32[]{:T(128)S(6)} %select_n.226, s32[]{:T(128)} %constant.197.clone.1, s32[]{:T(128)} %constant.197.clone.1) | dynamic-update-slice | bytes 131076 | tf_op jit(solution)/shard_map/dynamic_update_slice | solution.py:32
  103.4 2.4 %dynamic_update_slice.47 = bf16[16,64,512]{2,0,1:T(8,128)(2,1)S(1)} dynamic-update-slice(bf16[16,64,512]{2,0,1:T(8,128)(2,1)S(1)} %dynamic_update_slice.46, bf16[1,64,512]{2,0,1:T(2,128)(2,1)} %copy-done.2, s32[]{:T(128)S(6)} %select_n.230, s32[]{:T(128)} %constant.197.clone.1, s32[]{:T(128)} %constant.197.clone.1) | dynamic-update-slice | bytes 131076 | tf_op jit(solution)/shard_map/dynamic_update_slice | solution.py:32
  105.8 2.4 %dynamic_update_slice.48 = bf16[16,64,512]{2,0,1:T(8,128)(2,1)S(1)} dynamic-update-slice(bf16[16,64,512]{2,0,1:T(8,128)(2,1)S(1)} %dynamic_update_slice.47, bf16[1,64,512]{2,0,1:T(2,128)(2,1)} %copy-done.3, s32[]{:T(128)S(6)} %select_n.234, s32[]{:T(128)} %constant.197.clone.1, s32[]{:T(128)} %constant.197.clone.1) | dynamic-update-slice | bytes 131076 | tf_op jit(solution)/shard_map/dynamic_update_slice | solution.py:32
  110.6 2.4 %dynamic_update_slice.50 = bf16[16,64,512]{2,0,1:T(8,128)(2,1)S(1)} dynamic-update-slice(bf16[16,64,512]{2,0,1:T(8,128)(2,1)S(1)} %dynamic_update_slice.49, bf16[1,64,512]{2,0,1:T(2,128)(2,1)} %collective-permute-done.5, s32[]{:T(128)S(6)} %select_n.242, s32[]{:T(128)} %constant.197.clone.1, s32[]{:T(128)} %constant.197.clone.1) | dynamic-update-slice | bytes 131076 | tf_op jit(solution)/shard_map/dynamic_update_slice | solution.py:32
  113.0 2.4 %dynamic_update_slice.51 = bf16[16,64,512]{2,0,1:T(8,128)(2,1)S(1)} dynamic-update-slice(bf16[16,64,512]{2,0,1:T(8,128)(2,1)S(1)} %dynamic_update_slice.50, bf16[1,64,512]{2,0,1:T(2,128)(2,1)} %collective-permute-done.6, s32[]{:T(128)S(6)} %select_n.246, s32[]{:T(128)} %constant.197.clone.1, s32[]{:T(128)} %constant.197.clone.1) | dynamic-update-slice | bytes 131076 | tf_op jit(solution)/shard_map/dynamic_update_slice | solution.py:32
  115.3 2.4 %dynamic_update_slice.52 = bf16[16,64,512]{2,0,1:T(8,128)(2,1)S(1)} dynamic-update-slice(bf16[16,64,512]{2,0,1:T(8,128)(2,1)S(1)} %dynamic_update_slice.51, bf16[1,64,512]{2,0,1:T(2,128)(2,1)} %collective-permute-done.7, s32[]{:T(128)S(6)} %select_n.250, s32[]{:T(128)} %constant.197.clone.1, s32[]{:T(128)} %constant.197.clone.1) | dynamic-update-slice | bytes 131076 | tf_op jit(solution)/shard_map/dynamic_update_slice | solution.py:32
  117.7 2.4 %dynamic_update_slice.53 = bf16[16,64,512]{2,0,1:T(8,128)(2,1)S(1)} dynamic-update-slice(bf16[16,64,512]{2,0,1:T(8,128)(2,1)S(1)} %dynamic_update_slice.52, bf16[1,64,512]{2,0,1:T(2,128)(2,1)} %collective-permute-done.8, s32[]{:T(128)S(6)} %select_n.254, s32[]{:T(128)} %constant.197.clone.1, s32[]{:T(128)} %constant.197.clone.1) | dynamic-update-slice | bytes 131076 | tf_op jit(solution)/shard_map/dynamic_update_slice | solution.py:32
  135.6 7.8 %convolution_convert_fusion = bf16[256,8192]{1,0:T(8,128)(2,1)} fusion(bf16[512,8192]{1,0:T(8,128)(2,1)} %all-gather.2.cloned.1.call-done, bf16[32,8,4,128]{3,2,1,0:T(4,128)(2,1)S(1)} %bitcast.67), kind=kOutput, calls=%fused_computation.2 | convolution fusion | flops 2149580800 | bytes 12845056 | tf_op jit(solution)/shard_map/dot_general | solution.py:61
  143.4 65.9 %reduce-scatter.2.cloned.1.call-done = bf16[16,8192]{1,0:T(8,128)(2,1)} async-done(((bf16[256,8192]{1,0:T(8,128)(2,1)}), bf16[16,8192]{1,0:T(8,128)(2,1)}) %reduce-scatter.2.cloned.1.call-update) | async-done | bytes 262160 | tf_op jit(solution)/shard_map/reduce_scatter | solution.py:66
  (60 shorter events, 33.7 us)
Async XLA Ops:
  6.5 73.8 %copy-start.5 = (s32[4,2]{0,1:T(2,128)S(1)}, s32[4,2]{0,1:T(2,128)}, u32[]{:S(2)}) copy-start(s32[4,2]{0,1:T(2,128)} %param.9) | copy-start | bytes 100
  6.5 74.3 %copy-start.1 = (bf16[256,512]{1,0:T(8,128)(2,1)S(1)}, bf16[256,512]{1,0:T(8,128)(2,1)}, u32[]{:S(2)}) copy-start(bf16[256,512]{1,0:T(8,128)(2,1)} %param.6) | copy-start | bytes 786436
  6.5 129.1 %all-gather.2.cloned.1.call-start = ((), (), s32[]{:S(2)}) async-start(), calls=%async_computation.2 | async-start | bytes 8650752 | tf_op jit(solution)/shard_map/all_gather | solution.py:63
  9.7 123.5 %all-to-all-start = ((bf16[64,16,512]{2,0,1:T(8,128)(2,1)}), bf16[64,16,512]{2,0,1:T(8,128)(2,1)S(1)}, u32[]{:S(2)}, u32[]{:S(2)}) async-start(bf16[64,16,512]{2,0,1:T(8,128)(2,1)} %bitcast.58), calls=%async_computation | async-start | bytes 2097152 | tf_op jit(solution)/shard_map/all_to_all | solution.py:39
  20.1 189.2 %reduce-scatter.2.cloned.1.call-start = ((), (), s32[]{:S(2)}) async-start(), calls=%async_computation.3 | async-start | bytes 4456448 | tf_op jit(solution)/shard_map/reduce_scatter | solution.py:66
  25.1 24.2 %collective-permute-start = (bf16[1,64,512]{2,0,1:T(2,128)(2,1)S(1)}, bf16[1,64,512]{2,0,1:T(2,128)(2,1)}, u32[]{:S(2)}, u32[]{:S(2)}) collective-permute-start(bf16[1,64,512]{2,0,1:T(2,128)(2,1)S(1)} %get-tuple-element.19), channel_id=1, source_target_pairs={{0,1},{1,2},{2,3},{3,4},{4,5},{5,6},{6,7},{7,8},{8,9},{9,10},{10,1... | collective-permute-start | bytes 196616 | tf_op jit(solution)/shard_map/ppermute | solution.py:31
  25.5 26.9 %collective-permute-start.1 = (bf16[1,64,512]{2,0,1:T(2,128)(2,1)S(1)}, bf16[1,64,512]{2,0,1:T(2,128)(2,1)}, u32[]{:S(2)}, u32[]{:S(2)}) collective-permute-start(bf16[1,64,512]{2,0,1:T(2,128)(2,1)S(1)} %get-tuple-element.18), channel_id=1, source_target_pairs={{0,2},{1,3},{2,4},{3,5},{4,6},{5,7},{6,8},{7,9},{8,10},{9,11},{10,... | collective-permute-start | bytes 196616 | tf_op jit(solution)/shard_map/ppermute | solution.py:31
  29.1 27.8 %collective-permute-start.2 = (bf16[1,64,512]{2,0,1:T(2,128)(2,1)S(1)}, bf16[1,64,512]{2,0,1:T(2,128)(2,1)S(1)}, u32[]{:S(2)}, u32[]{:S(2)}) collective-permute-start(bf16[1,64,512]{2,0,1:T(2,128)(2,1)S(1)} %get-tuple-element.17), channel_id=1, source_target_pairs={{0,3},{1,4},{2,5},{3,6},{4,7},{5,8},{6,9},{7,10},{8,11},{9,12},{10... | collective-permute-start | bytes 196616 | tf_op jit(solution)/shard_map/ppermute | solution.py:31
  33.2 27.7 %collective-permute-start.3 = (bf16[1,64,512]{2,0,1:T(2,128)(2,1)S(1)}, bf16[1,64,512]{2,0,1:T(2,128)(2,1)S(1)}, u32[]{:S(2)}, u32[]{:S(2)}) collective-permute-start(bf16[1,64,512]{2,0,1:T(2,128)(2,1)S(1)} %get-tuple-element.16), channel_id=1, source_target_pairs={{0,4},{1,5},{2,6},{3,7},{4,8},{5,9},{6,10},{7,11},{8,12},{9,13},{1... | collective-permute-start | bytes 196616 | tf_op jit(solution)/shard_map/ppermute | solution.py:31
  37.8 38.5 %collective-permute-start.4 = (bf16[1,64,512]{2,0,1:T(2,128)(2,1)S(1)}, bf16[1,64,512]{2,0,1:T(2,128)(2,1)S(1)}, u32[]{:S(2)}, u32[]{:S(2)}) collective-permute-start(bf16[1,64,512]{2,0,1:T(2,128)(2,1)S(1)} %get-tuple-element.15), channel_id=1, source_target_pairs={{0,5},{1,6},{2,7},{3,8},{4,9},{5,10},{6,11},{7,12},{8,13},{9,14},{... | collective-permute-start | bytes 196616 | tf_op jit(solution)/shard_map/ppermute | solution.py:31
  49.3 31.7 %collective-permute-start.5 = (bf16[1,64,512]{2,0,1:T(2,128)(2,1)}, bf16[1,64,512]{2,0,1:T(2,128)(2,1)}, u32[]{:S(2)}, u32[]{:S(2)}) collective-permute-start(bf16[1,64,512]{2,0,1:T(2,128)(2,1)} %get-tuple-element.14), channel_id=1, source_target_pairs={{0,6},{1,7},{2,8},{3,9},{4,10},{5,11},{6,12},{7,13},{8,14},{9,15},... | collective-permute-start | bytes 196616 | tf_op jit(solution)/shard_map/ppermute | solution.py:31
  52.4 33.7 %collective-permute-start.6 = (bf16[1,64,512]{2,0,1:T(2,128)(2,1)}, bf16[1,64,512]{2,0,1:T(2,128)(2,1)}, u32[]{:S(2)}, u32[]{:S(2)}) collective-permute-start(bf16[1,64,512]{2,0,1:T(2,128)(2,1)} %get-tuple-element.13), channel_id=1, source_target_pairs={{0,7},{1,8},{2,9},{3,10},{4,11},{5,12},{6,13},{7,14},{8,15},{9,0},... | collective-permute-start | bytes 196616 | tf_op jit(solution)/shard_map/ppermute | solution.py:31
  56.9 19.5 %copy-start.2 = (bf16[1,64,512]{2,0,1:T(2,128)(2,1)}, bf16[1,64,512]{2,0,1:T(2,128)(2,1)S(1)}, u32[]{:S(2)}) copy-start(bf16[1,64,512]{2,0,1:T(2,128)(2,1)S(1)} %collective-permute-done.2) | copy-start | bytes 196612
  56.9 37.1 %collective-permute-start.7 = (bf16[1,64,512]{2,0,1:T(2,128)(2,1)}, bf16[1,64,512]{2,0,1:T(2,128)(2,1)}, u32[]{:S(2)}, u32[]{:S(2)}) collective-permute-start(bf16[1,64,512]{2,0,1:T(2,128)(2,1)} %get-tuple-element.12), channel_id=1, source_target_pairs={{0,8},{1,9},{2,10},{3,11},{4,12},{5,13},{6,14},{7,15},{8,0},{9,1},... | collective-permute-start | bytes 196616 | tf_op jit(solution)/shard_map/ppermute | solution.py:31
  60.9 15.4 %copy-start.3 = (bf16[1,64,512]{2,0,1:T(2,128)(2,1)}, bf16[1,64,512]{2,0,1:T(2,128)(2,1)S(1)}, u32[]{:S(2)}) copy-start(bf16[1,64,512]{2,0,1:T(2,128)(2,1)S(1)} %collective-permute-done.3) | copy-start | bytes 196612
  61.0 35.2 %collective-permute-start.8 = (bf16[1,64,512]{2,0,1:T(2,128)(2,1)S(1)}, bf16[1,64,512]{2,0,1:T(2,128)(2,1)}, u32[]{:S(2)}, u32[]{:S(2)}) collective-permute-start(bf16[1,64,512]{2,0,1:T(2,128)(2,1)S(1)} %get-tuple-element.11), channel_id=1, source_target_pairs={{0,9},{1,10},{2,11},{3,12},{4,13},{5,14},{6,15},{7,0},{8,1},{9,2},... | collective-permute-start | bytes 196616 | tf_op jit(solution)/shard_map/ppermute | solution.py:31
  76.3 0.7 copy-start.4
  77.0 21.3 %collective-permute-start.9 = (bf16[1,64,512]{2,0,1:T(2,128)(2,1)S(1)}, bf16[1,64,512]{2,0,1:T(2,128)(2,1)}, u32[]{:S(2)}, u32[]{:S(2)}) collective-permute-start(bf16[1,64,512]{2,0,1:T(2,128)(2,1)S(1)} %get-tuple-element.10), channel_id=1, source_target_pairs={{0,10},{1,11},{2,12},{3,13},{4,14},{5,15},{6,0},{7,1},{8,2},{9,3},... | collective-permute-start | bytes 196616 | tf_op jit(solution)/shard_map/ppermute | solution.py:31
  81.0 41.5 %collective-permute-start.10 = (bf16[1,64,512]{2,0,1:T(2,128)(2,1)S(1)}, bf16[1,64,512]{2,0,1:T(2,128)(2,1)S(1)}, u32[]{:S(2)}, u32[]{:S(2)}) collective-permute-start(bf16[1,64,512]{2,0,1:T(2,128)(2,1)S(1)} %get-tuple-element.9), channel_id=1, source_target_pairs={{0,11},{1,12},{2,13},{3,14},{4,15},{5,0},{6,1},{7,2},{8,3},{9,4},{... | collective-permute-start | bytes 196616 | tf_op jit(solution)/shard_map/ppermute | solution.py:31
  86.2 37.6 %collective-permute-start.11 = (bf16[1,64,512]{2,0,1:T(2,128)(2,1)S(1)}, bf16[1,64,512]{2,0,1:T(2,128)(2,1)S(1)}, u32[]{:S(2)}, u32[]{:S(2)}) collective-permute-start(bf16[1,64,512]{2,0,1:T(2,128)(2,1)S(1)} %get-tuple-element.8), channel_id=1, source_target_pairs={{0,12},{1,13},{2,14},{3,15},{4,0},{5,1},{6,2},{7,3},{8,4},{9,5},{1... | collective-permute-start | bytes 196616 | tf_op jit(solution)/shard_map/ppermute | solution.py:31
  94.0 31.0 %collective-permute-start.12 = (bf16[1,64,512]{2,0,1:T(2,128)(2,1)S(1)}, bf16[1,64,512]{2,0,1:T(2,128)(2,1)}, u32[]{:S(2)}, u32[]{:S(2)}) collective-permute-start(bf16[1,64,512]{2,0,1:T(2,128)(2,1)S(1)} %get-tuple-element.7), channel_id=1, source_target_pairs={{0,13},{1,14},{2,15},{3,0},{4,1},{5,2},{6,3},{7,4},{8,5},{9,6},{10... | collective-permute-start | bytes 196616 | tf_op jit(solution)/shard_map/ppermute | solution.py:31
  96.2 31.2 %collective-permute-start.13 = (bf16[1,64,512]{2,0,1:T(2,128)(2,1)S(1)}, bf16[1,64,512]{2,0,1:T(2,128)(2,1)S(1)}, u32[]{:S(2)}, u32[]{:S(2)}) collective-permute-start(bf16[1,64,512]{2,0,1:T(2,128)(2,1)S(1)} %get-tuple-element.6), channel_id=1, source_target_pairs={{0,14},{1,15},{2,0},{3,1},{4,2},{5,3},{6,4},{7,5},{8,6},{9,7},{10,... | collective-permute-start | bytes 196616 | tf_op jit(solution)/shard_map/ppermute | solution.py:31
  98.3 30.3 %collective-permute-start.14 = (bf16[1,64,512]{2,0,1:T(2,128)(2,1)S(1)}, bf16[1,64,512]{2,0,1:T(2,128)(2,1)S(1)}, u32[]{:S(2)}, u32[]{:S(2)}) collective-permute-start(bf16[1,64,512]{2,0,1:T(2,128)(2,1)S(1)} %get-tuple-element.5), channel_id=1, source_target_pairs={{0,15},{1,0},{2,1},{3,2},{4,3},{5,4},{6,5},{7,6},{8,7},{9,8},{10,9... | collective-permute-start | bytes 196616 | tf_op jit(solution)/shard_map/ppermute | solution.py:31
  135.6 73.7 %copy-start = (bf16[16,8192]{1,0:T(8,128)(2,1)S(1)}, bf16[16,8192]{1,0:T(8,128)(2,1)}, u32[]{:S(2)}) copy-start(bf16[16,8192]{1,0:T(8,128)(2,1)} %param.10) | copy-start | bytes 786436
Sparse Core Ops, SparseCore 0:
  10.4 112.3 all-gather.1
  143.5 65.7 reduce-scatter.1
